TPU v7x, 256 devices: a whole 4x4x8 slice. The times are simulated.
256 devices in a mesh: row: 16 (over y, x), col: 8 (over z), vox: 2 (over core).
Axes of the slice: x: 4, y: 4, z: 8, core: 2. Of those that a mesh axis runs over, the one named last changes fastest.
Arguments:
- coeffs_r: bfloat16 [32, 16, 64, 2, 1024], P(None, 'row', None, None, 'col'), may hold values from -0.125 to 0.125
- rhs: bfloat16 [32, 16, 64, 1536], P('col', 'row', None, 'vox'), may hold values from -6 to 6
- inverses: bfloat16 [2, 1024, 1024], replicated, may hold values from -0.1875 to 0.1875
Outputs:
- updated: bfloat16 [32, 16, 64, 1536], P('col', 'row', None, 'vox')
All inputs are finite; a program needn't handle non-finite values.
Results may differ from a plain program's by a relative error of at most 0.0049.
Values may be sent and summed in bfloat16 or wider, within the bound.
A program may use at most 64 MiB of HBM per device.

v0:
```python
import jax
import jax.numpy as jnp
from jax import lax
from jax.sharding import PartitionSpec as P


def spread(value, axis, root):
    mine = lax.axis_index(axis) == root
    return lax.psum(jnp.where(mine, value, jnp.zeros_like(value)), axis)


def solve_block(inverse, rhs_block, col_pos, own_cols):
    solved_all = jnp.dot(inverse, rhs_block, preferred_element_type=jnp.float32).astype(
        jnp.bfloat16
    )
    solved_mine = lax.dynamic_slice_in_dim(solved_all, col_pos * own_cols, own_cols, 0)
    return (solved_all, solved_mine)


def local(coeffs_r, rhs, inverses):
    row_count = lax.axis_size("row")
    col_count = lax.axis_size("col")
    row_pos = lax.axis_index("row")
    col_pos = lax.axis_index("col")
    per_col = rhs.shape[0]
    block_rows = rhs.shape[2]
    voxels = rhs.shape[3]
    cycles = coeffs_r.shape[0]
    own_cols = coeffs_r.shape[4]
    block_order = inverses.shape[1]
    tail_cycles = block_order // (block_rows * row_count)
    owner_col = col_count - 1
    tail_piece = rhs[per_col - tail_cycles :]
    tail_rows = lax.all_gather(tail_piece, "row", axis=1, tiled=True)
    tail_rows = spread(tail_rows, "col", owner_col)
    solved_last, last_mine = solve_block(
        inverses[1], tail_rows.reshape(block_order, voxels), col_pos, own_cols
    )
    panel_rows = coeffs_r[cycles - 2 * tail_cycles : cycles - tail_cycles, 0, :, 1, :]
    panel_rows = panel_rows.reshape(tail_cycles * block_rows, own_cols)
    partial_value = -jnp.dot(panel_rows, last_mine, preferred_element_type=jnp.float32)
    known = rhs[per_col - 2 * tail_cycles : per_col - tail_cycles, 0]
    known = known.reshape(tail_cycles * block_rows, voxels).astype(jnp.float32)
    partial_value = partial_value + jnp.where(col_pos == owner_col, known, jnp.zeros_like(known))
    partial_value = partial_value.reshape(tail_cycles, 1, block_rows, voxels)
    padded = jnp.zeros((tail_cycles, row_count, block_rows, voxels), jnp.float32)
    anchor = jnp.zeros((), jnp.int32)
    padded = lax.dynamic_update_slice(padded, partial_value, (anchor, row_pos, anchor, anchor))
    middle_rhs = lax.psum(padded, ("row", "col")).astype(jnp.bfloat16)
    solved_first, first_mine = solve_block(
        inverses[0], middle_rhs.reshape(block_order, voxels), col_pos, own_cols
    )
    stacked_mine = jnp.stack([first_mine, last_mine])
    removed = lax.psum_scatter(
        jnp.einsum("kprjc,jcv->kprv", coeffs_r, stacked_mine, preferred_element_type=jnp.float32),
        "col",
        scatter_dimension=0,
        tiled=True,
    )
    remaining = (rhs.astype(jnp.float32) - removed).astype(jnp.bfloat16)

    def my_rows(solved):
        shaped = solved.reshape(tail_cycles, row_count, block_rows, voxels)
        return lax.dynamic_slice_in_dim(shaped, row_pos, 1, 1)

    window = jnp.concatenate([my_rows(solved_first), my_rows(solved_last)], 0)
    lower_part = jnp.where(col_pos == owner_col, window, remaining[per_col - 2 * tail_cycles :])
    return jnp.concatenate([remaining[: per_col - 2 * tail_cycles], lower_part], 0)


def solution(mesh):
    placed = (P(None, "row", None, None, "col"), P("col", "row", None, "vox"), P())
    return jax.shard_map(
        local, mesh=mesh, in_specs=placed, out_specs=P("col", "row", None, "vox"), check_vma=False
    )
```

profile of v0, /device:TPU:1, one launch (start us, length us, event | category | flops | bytes accessed | tf_op | source)
XLA Modules:
  0.0 951.8 jit_solution(15609546226498273052)
XLA Ops:
  6.5 0.0 all-gather.2.cloned.1.call-start
  6.5 1.5 slice.28
  8.1 0.0 all-gather.2.cloned.1.call-update
  8.1 0.0 all-reduce.3.cloned.1.call-start
  8.2 53.5 %all-gather.2.cloned.1.call-done = bf16[1,16,64,768]{3,2,0,1:T(8,128)(2,1)} async-done(((bf16[1,1,64,768]{3,2,0,1:T(8,128)(2,1)}), bf16[1,16,64,768]{3,2,0,1:T(8,128)(2,1)}) %all-gather.2.cloned.1.call-update) | async-done | bytes 1572880 | tf_op jit(solution)/shard_map/all_gather | solution.py:34
  61.6 1.3 broadcast_select_fusion
  62.9 0.0 all-reduce.3.cloned.1.call-update
  62.9 0.0 reduce-scatter.2.cloned.1.call-start
  63.0 1.4 slice.23
  64.4 75.1 %all-reduce.3.cloned.1.call-done = bf16[1024,768]{1,0:T(8,128)(2,1)} async-done(((bf16[1024,768]{1,0:T(8,128)(2,1)}), bf16[1024,768]{1,0:T(8,128)(2,1)}) %all-reduce.3.cloned.1.call-update) | async-done | bytes 1572880 | tf_op jit(solution)/shard_map/psum | solution.py:9
  139.5 3.9 fusion.6
  143.4 0.0 copy-start
  143.4 0.8 dynamic-slice_bitcast_fusion.1
  144.3 0.0 copy-start.3
  144.3 0.0 copy-start.5
  144.3 0.3 broadcast_in_dim.9
  144.6 0.0 copy-done
  144.6 0.6 copy-done.3
  145.2 0.0 copy-done.5
  145.2 0.2 fusion.15
  145.5 610.3 %all-reduce.4 = bf16[1,16,64,768]{3,2,1,0:T(8,128)(2,1)} all-reduce(f32[1,16,64,768]{3,2,1,0:T(8,128)S(1)} %fusion.15), channel_id=1, replica_groups=mesh['row'=16,'col'=8,'vox'=2] {'row','col'}, use_global_device_ids=true, to_apply=%region_1.2 | all-reduce | flops 786432 | bytes 4718592 | tf_op jit(solution)/shard_map/psum | solution.py:49
  755.8 0.0 copy-start.2
  755.8 0.0 copy-start.4
  755.8 4.0 fusion.9
  759.8 0.1 dynamic-slice_bitcast_fusion
  759.9 0.0 copy-done.2
  759.9 0.0 copy-done.4
  759.9 3.7 convolution_bitcast_fusion
  763.6 0.0 copy-start.1
  763.6 0.0 reduce-scatter.2.cloned.1.call-update
  763.6 1.4 copy-done.1
  765.0 1.6 copy.26
  766.5 0.7 copy.24
  767.2 0.9 constant_dynamic-slice_fusion
  768.1 175.1 %reduce-scatter.2.cloned.1.call-done = f32[4,1,64,768]{3,2,0,1:T(8,128)} async-done(((f32[32,1,64,768]{3,2,0,1:T(8,128)}), f32[4,1,64,768]{3,2,0,1:T(8,128)}) %reduce-scatter.2.cloned.1.call-update) | async-done | bytes 786448 | tf_op jit(solution)/shard_map/reduce_scatter | solution.py:54
  943.3 1.2 subtract_convert_fusion
  944.5 0.8 maximum_bitcast_fusion.2
  (2 shorter events, 0.0 us)
Async XLA Ops:
  6.5 55.1 %all-gather.2.cloned.1.call-start = ((), (), s32[]{:S(2)}) async-start(), calls=%async_computation.1 | async-start | bytes 1671168 | tf_op jit(solution)/shard_map/all_gather | solution.py:34
  8.1 131.4 %all-reduce.3.cloned.1.call-start = ((), (), s32[]{:S(2)}) async-start(), calls=%async_computation.2 | async-start | bytes 3145728 | tf_op jit(solution)/shard_map/psum | solution.py:9
  62.9 880.4 %reduce-scatter.2.cloned.1.call-start = ((), (), s32[]{:S(2)}) async-start(), calls=%async_computation.3 | async-start | bytes 7077888 | tf_op jit(solution)/shard_map/reduce_scatter | solution.py:54
  143.4 1.2 copy-start
  144.3 1.0 copy-start.3
  144.3 1.0 copy-start.5
  755.8 4.1 copy-start.2
  755.8 4.1 copy-start.4
  763.6 1.4 copy-start.1
Sparse Core Ops, SparseCore 0:
  9.8 51.8 all-gather.1
  64.0 75.4 all-reduce.2
  763.7 179.5 reduce-scatter.1
where the time goes:
time: 952 us
  blocking collectives  610 us (64%)
  waiting for transfers between devices  304 us (32%)
  between operations  13.2 us (1%)
  matrix products  11.8 us (1%)
    psum x1, blocking collectives, local(): middle_rhs = lax.psum(padded, ('row', 'col')).astype(jnp.bfloat16)  610 us
    reduce_scatter x1, waiting for transfers between devices, local(): lax.psum_scatter(jnp.einsum('kprjc,jcv->kprv', coeffs_r, stacked_mine, pr...  175 us
    psum x1, waiting for transfers between devices, spread(): return lax.psum(jnp.where(mine, value, jnp.zeros_like(value)), axis)  75.1 us
    all_gather x1, waiting for transfers between devices, local(): tail_rows = lax.all_gather(tail_piece, 'row', axis=1, tiled=True)  53.5 us
  transfers between devices with their start and end apart: 3, of which 3 were waited for; matrix products, arithmetic and copies ran while one was open for 0% of the time, Pallas kernels for 0%

commit v1 on v0

v1 whole, which is shorter than its diff:
```python
import jax
import jax.numpy as jnp
from jax import lax
from jax.experimental import pallas as pl
from jax.experimental.pallas import tpu as pltpu
from jax.sharding import PartitionSpec as P

MESH = pl.DeviceIdType.MESH
BF = jnp.bfloat16
F32 = jnp.float32
X, Y, Z = 4, 4, 8
CHUNKS, WIDTH = 3, 256
ROWS = 64
HALF = ROWS // 2
OWN = 128
ORDER = 1024
LAST = Z - 1


def dot(a, b):
    return jnp.dot(a, b, preferred_element_type=F32)


def split_pairs():
    r = lax.broadcasted_iota(jnp.int32, (2 * ROWS, 2 * ROWS), 0)
    c = lax.broadcasted_iota(jnp.int32, (2 * ROWS, 2 * ROWS), 1)
    wanted = jnp.where(r < ROWS, 2 * r, 2 * (r - ROWS) + 1)
    return jnp.where(c == wanted, 1.0, 0.0).astype(BF)


def kernel(
    coeffs,
    rhs,
    inverses,
    out,
    inv,
    mine,
    paired,
    mid_raw,
    factor,
    panel,
    known,
    tail,
    middle,
    solved_last,
    solved_mid,
    acc,
    local_sem,
    z_send,
    z_recv,
    k_send,
    k_recv,
    p_send,
    p_recv,
    c_send,
    c_recv,
    s_send,
    s_recv,
    g_send,
    g_recv,
):
    row = lax.axis_index("row")
    z = lax.axis_index("col")
    core = lax.axis_index("vox")
    x, y = lax.rem(row, X), row // X

    def at_z(d):
        return (row, lax.rem(z + d, Z), core)

    def at_x(d):
        return (y * X + lax.rem(x + d, X), z, core)

    def at_y(d):
        return (lax.rem(y + d, Y) * X + x, z, core)

    sibling = (row, z, 1 - core)

    def remote(src, dst, send, recv, where):
        return pltpu.make_async_remote_copy(
            src_ref=src, dst_ref=dst, send_sem=send, recv_sem=recv, device_id=where, device_id_type=MESH
        )

    def columns(j):
        return pl.ds(j * WIDTH, WIDTH)

    load_rhs = pltpu.make_async_copy(rhs, mine, local_sem.at[0])
    load_mid = pltpu.make_async_copy(coeffs.at[30], mid_raw, local_sem.at[1])
    load_inv1 = pltpu.make_async_copy(inverses.at[1], inv.at[1], local_sem.at[2])
    load_own = pltpu.make_async_copy(coeffs.at[pl.ds(4 * z, 4)], paired.at[z], local_sem.at[3])
    load_inv0 = pltpu.make_async_copy(inverses.at[0], inv.at[0], local_sem.at[4])
    for load in (load_rhs, load_mid, load_inv1, load_own, load_inv0):
        load.start()

    barrier = pltpu.get_barrier_semaphore()
    peers = [at_z(d) for d in range(1, Z)] + [at_x(d) for d in range(1, X)] + [at_y(d) for d in range(1, Y)] + [sibling]
    for peer in peers:
        pl.semaphore_signal(barrier, inc=1, device_id=peer, device_id_type=MESH)
    load_rhs.wait()
    load_mid.wait()
    pick = split_pairs()
    panel_mine = dot(pick[ROWS:], mid_raw[...]).astype(BF)
    panel[z] = panel_mine
    pl.semaphore_wait(barrier, len(peers))

    def tail_copy(j, d):
        return remote(mine.at[3, :, columns(j)], tail.at[j, y, x], z_send.at[j, d - 1], z_recv.at[j], at_z(d))

    def known_copy(d):
        return remote(mine.at[2], known, k_send.at[d - 1], k_recv, at_z(d))

    def panel_copy(d):
        return remote(panel.at[z], panel.at[z], p_send.at[d - 1], p_recv.at[d - 1], at_z(d))

    order = (4, 3, 5, 2, 6, 1, 7)

    @pl.when(z == LAST)
    def _():
        for d in order:
            tail_copy(0, d).start()

    for d in order:
        panel_copy(d).start()

    @pl.when(z == LAST)
    def _():
        for j in range(1, CHUNKS):
            for d in order:
                tail_copy(j, d).start()
        for d in order:
            known_copy(d).start()
        for j in range(CHUNKS):
            tail[j, y, x] = mine[3, :, j * WIDTH : (j + 1) * WIDTH]
        known[...] = mine[2]

    upper, lower = pl.ds(0, HALF), pl.ds(HALF, HALF)

    def gather(which, buf, j, stage, half, d):
        send, recv = g_send.at[which, j, stage, half, d - 1], g_recv.at[which, j, stage, half, d - 1]
        if stage == 0:
            rows = upper if half == 0 else lower
            part, where = buf.at[j, y, x, rows], (at_x(d) if half == 0 else at_y(d))
        elif half == 0:
            part, where = buf.at[j, y, :, upper], at_y(d)
        else:
            part, where = buf.at[j, :, x, lower], at_x(d)
        return remote(part, part, send, recv, where)

    every = [(half, d) for d in (2, 1, 3) for half in (0, 1)]

    def start(which, buf, j, stage):
        for half, d in every:
            gather(which, buf, j, stage, half, d).start()

    def arrive(which, buf, j, stage):
        for half, d in every:
            gather(which, buf, j, stage, half, d).wait_recv()

    def tail_here(j):
        @pl.when(z != LAST)
        def _():
            tail_copy(j, 1).wait_recv()

        start(0, tail, j, 0)

    def coeff_copy(d):
        to = lax.rem(z + d, Z)
        return remote(
            coeffs.at[pl.ds(4 * to + 2 * core, 2)],
            paired.at[z, pl.ds(2 * core, 2)],
            c_send.at[d - 1],
            c_recv.at[d - 1],
            at_z(d),
        )

    def share_copy(d):
        part = paired.at[lax.rem(z + Z - d, Z), pl.ds(2 * core, 2)]
        return remote(part, part, s_send.at[d - 1], s_recv.at[d - 1], sibling)

    tail_here(0)
    tail_here(1)
    arrive(0, tail, 0, 0)
    start(0, tail, 0, 1)
    tail_here(2)
    for d in order:
        coeff_copy(d).start()
    arrive(0, tail, 1, 0)
    start(0, tail, 1, 1)
    arrive(0, tail, 2, 0)
    start(0, tail, 2, 1)

    load_inv1.wait()
    for d in order:
        panel_copy(d).wait_recv()

    @pl.when(z != LAST)
    def _():
        known_copy(1).wait_recv()

    panel_full = jnp.concatenate([panel[c] for c in range(Z)], axis=1)

    def solve_last(j):
        arrive(0, tail, j, 1)
        block = tail[j].reshape(ORDER, WIDTH)
        solved = dot(inv[1], block).astype(BF)
        solved_last[j] = solved
        part = known[:, j * WIDTH : (j + 1) * WIDTH].astype(F32) - dot(panel_full, solved)
        middle[j, y, x] = part.astype(BF)
        start(1, middle, j, 0)

    def pass_on(j):
        arrive(1, middle, j, 0)
        start(1, middle, j, 1)

    solve_last(0)
    solve_last(1)
    pass_on(0)
    solve_last(2)
    pass_on(1)
    for d in order:
        coeff_copy(d).wait_recv()
        share_copy(d).start()
    pass_on(2)
    load_own.wait()
    load_inv0.wait()
    for d in order:
        share_copy(d).wait_recv()
    for k in range(4):
        both = dot(pick, jnp.concatenate([paired[c, k] for c in range(Z)], axis=1)).astype(BF)
        factor[0, k * ROWS : (k + 1) * ROWS] = both[:ROWS]
        factor[1, k * ROWS : (k + 1) * ROWS] = both[ROWS:]
    for j in range(CHUNKS):
        here = mine[:, :, j * WIDTH : (j + 1) * WIDTH].reshape(4 * ROWS, WIDTH).astype(F32)
        acc[j] = here - dot(factor[1], solved_last[j])
    own_rows = pl.ds(pl.multiple_of(row * ROWS, ROWS), ROWS)
    for j in range(CHUNKS):
        arrive(1, middle, j, 1)
        solved = dot(inv[0], middle[j].reshape(ORDER, WIDTH)).astype(BF)
        solved_mid[...] = solved
        result = (acc[j] - dot(factor[0], solved)).astype(BF)
        out[:, :, j * WIDTH : (j + 1) * WIDTH] = result.reshape(4, ROWS, WIDTH)

        @pl.when(z == LAST)
        def _():
            out[2, :, j * WIDTH : (j + 1) * WIDTH] = solved_mid[own_rows]
            out[3, :, j * WIDTH : (j + 1) * WIDTH] = solved_last[j, own_rows]

    @pl.when(z == LAST)
    def _():
        for d in order:
            for j in range(CHUNKS):
                tail_copy(j, d).wait_send()
            known_copy(d).wait_send()

    for d in order:
        panel_copy(d).wait_send()
        coeff_copy(d).wait_send()
        share_copy(d).wait_send()
    for which, buf in ((0, tail), (1, middle)):
        for j in range(CHUNKS):
            for stage in range(2):
                for half, d in every:
                    gather(which, buf, j, stage, half, d).wait_send()


def local(coeffs_r, rhs, inverses):
    cycles = coeffs_r.shape[0]
    any_space = pl.BlockSpec(memory_space=pl.ANY)
    dma = pltpu.SemaphoreType.DMA
    out = pl.pallas_call(
        kernel,
        out_shape=jax.ShapeDtypeStruct((4, ROWS, CHUNKS * WIDTH), BF),
        in_specs=[any_space] * 3,
        out_specs=pl.BlockSpec(memory_space=pltpu.VMEM),
        scratch_shapes=[
            pltpu.VMEM((2, ORDER, ORDER), BF),
            pltpu.VMEM((4, ROWS, CHUNKS * WIDTH), BF),
            pltpu.VMEM((Z, 4, 2 * ROWS, OWN), BF),
            pltpu.VMEM((2 * ROWS, OWN), BF),
            pltpu.VMEM((2, 4 * ROWS, ORDER), BF),
            pltpu.VMEM((Z, ROWS, OWN), BF),
            pltpu.VMEM((ROWS, CHUNKS * WIDTH), BF),
            pltpu.VMEM((CHUNKS, Y, X, ROWS, WIDTH), BF),
            pltpu.VMEM((CHUNKS, Y, X, ROWS, WIDTH), BF),
            pltpu.VMEM((CHUNKS, ORDER, WIDTH), BF),
            pltpu.VMEM((ORDER, WIDTH), BF),
            pltpu.VMEM((CHUNKS, 4 * ROWS, WIDTH), F32),
            dma((5,)),
            dma((CHUNKS, Z - 1)),
            dma((CHUNKS,)),
            dma((Z - 1,)),
            dma,
            dma((Z - 1,)),
            dma((Z - 1,)),
            dma((Z - 1,)),
            dma((Z - 1,)),
            dma((Z - 1,)),
            dma((Z - 1,)),
            dma((2, CHUNKS, 2, 2, 3)),
            dma((2, CHUNKS, 2, 2, 3)),
        ],
        compiler_params=pltpu.CompilerParams(
            collective_id=0, has_side_effects=True, vmem_limit_bytes=60 * 1024 * 1024
        ),
    )(
        coeffs_r.reshape(cycles, 2 * ROWS, OWN),
        rhs.reshape(4, ROWS, CHUNKS * WIDTH),
        inverses,
    )
    return out.reshape(rhs.shape)


def solution(mesh):
    placed = (P(None, "row", None, None, "col"), P("col", "row", None, "vox"), P())
    return jax.shard_map(
        local, mesh=mesh, in_specs=placed, out_specs=P("col", "row", None, "vox"), check_vma=False
    )
```

time: 952 us -> 55.5 us (0.06)
  the two profiles are of different devices: /device:TPU:1 before, /device:TPU:2 now
where the time goes in v1:
time: 55.5 us; the launch traced here: 55.4 us
  Pallas kernels  53.6 us (97%)
  local copies, waits for them, and re-layouts  1.77 us (3%)
    pallas_call x1, Pallas kernels, local(): pl.pallas_call(kernel, out_shape=jax.ShapeDtypeStruct((4, ROWS, CHUNKS *...  53.6 us
    unnamed x1, local copies, waits for them, and re-layouts  1.77 us

profile of v1, /device:TPU:2, one launch (start us, length us, event | category | flops | bytes accessed | tf_op | source)
XLA Modules:
  0.0 55.4 jit_solution(8376154700465664127)
XLA Ops:
  0.0 53.6 %shard_map.37 = bf16[4,64,768]{2,1,0:T(8,128)(2,1)} custom-call(bf16[32,128,128]{2,1,0:T(8,128)(2,1)} %bitcast.6, bf16[4,64,768]{2,1,0:T(8,128)(2,1)} %bitcast.7, bf16[2,1024,1024]{2,1,0:T(8,128)(2,1)} %inverses.1), custom_call_target="tpu_custom_call" | custom-call | tf_op jit(solution)/shard_map/pallas_call | solution.py:269
  53.6 1.8 %copy.6 = bf16[4,1,64,768]{3,2,1,0:T(8,128)(2,1)} copy(bf16[4,1,64,768]{3,2,1,0:T(8,128)(2,1)} %bitcast.5) | data formatting | bytes 786432

commit v2 on v1

v2 whole, which is shorter than its diff:
```python
import jax
import jax.numpy as jnp
from jax import lax
from jax.experimental import pallas as pl
from jax.experimental.pallas import tpu as pltpu
from jax.sharding import PartitionSpec as P

MESH = pl.DeviceIdType.MESH
BF = jnp.bfloat16
F32 = jnp.float32
X, Y, Z = 4, 4, 8
SIDE = 384
WIDTHS = (256, 128)
STARTS = (0, 256)
CHUNKS = len(WIDTHS)
ROWS = 64
HALF = ROWS // 2
OWN = 128
ORDER = 1024
LAST = Z - 1
FAR_FIRST = (4, 3, 5, 2, 6, 1, 7)


def dot(a, b):
    return jnp.dot(a, b, preferred_element_type=F32)


def picker(rows, wanted):
    r = lax.broadcasted_iota(jnp.int32, (rows, 2 * ROWS), 0)
    c = lax.broadcasted_iota(jnp.int32, (rows, 2 * ROWS), 1)
    return jnp.where(c == wanted(r), 1.0, 0.0).astype(BF)


def kernel(
    coeffs,
    rhs,
    inverses,
    out,
    inv,
    here,
    paired,
    mid_raw,
    factor,
    panel,
    known,
    tail0,
    tail1,
    middle0,
    middle1,
    last0,
    last1,
    solved0,
    solved1,
    acc0,
    acc1,
    res0,
    res1,
    local_sem,
    out_sem,
    t_send,
    t_recv,
    k_send,
    k_recv,
    h_send,
    h_recv,
    p_send,
    p_recv,
    q_send,
    q_recv,
    r_send,
    r_recv,
    s_send,
    s_recv,
    g_send,
    g_recv,
    o_send,
    o_recv,
):
    row = lax.axis_index("row")
    z = lax.axis_index("col")
    core = lax.axis_index("vox")
    x, y = lax.rem(row, X), row // X
    odd = lax.rem(z, 2)
    toward = 1 - 2 * odd
    tail, middle, last = (tail0, tail1), (middle0, middle1), (last0, last1)
    solved_mid, acc, res = (solved0, solved1), (acc0, acc1), (res0, res1)

    def turn(d):
        return lax.rem(z + 2 * Z + d, Z)

    def at_z(d):
        return (row, turn(d), core)

    def at_x(d):
        return (y * X + lax.rem(x + d, X), z, core)

    def at_y(d):
        return (lax.rem(y + d, Y) * X + x, z, core)

    partner = at_z(toward)
    sibling = (row, z, 1 - core)

    def remote(src, dst, send, recv, where):
        return pltpu.make_async_remote_copy(
            src_ref=src, dst_ref=dst, send_sem=send, recv_sem=recv, device_id=where, device_id_type=MESH
        )

    def side(h, j):
        return pl.ds(h * SIDE + STARTS[j], WIDTHS[j])

    my_side = pl.ds(pl.multiple_of(odd * SIDE, OWN), SIDE)
    other_side = pl.ds(pl.multiple_of((1 - odd) * SIDE, OWN), SIDE)
    pair_cycles = 8 * (z // 2)

    load_mid = pltpu.make_async_copy(coeffs.at[30], mid_raw, local_sem.at[0])
    load_inv1 = pltpu.make_async_copy(inverses.at[1], inv.at[1], local_sem.at[1])
    load_own = pltpu.make_async_copy(coeffs.at[pl.ds(pair_cycles, 8)], paired.at[z], local_sem.at[2])
    load_here = pltpu.make_async_copy(rhs.at[:, :, my_side], here.at[odd], local_sem.at[3])
    load_inv0 = pltpu.make_async_copy(inverses.at[0], inv.at[0], local_sem.at[4])
    load_tail = [
        pltpu.make_async_copy(rhs.at[3, :, side(1, j)], tail[j].at[y, x], local_sem.at[5 + j]) for j in range(CHUNKS)
    ]
    load_known = pltpu.make_async_copy(rhs.at[2, :, pl.ds(SIDE, SIDE)], known, local_sem.at[5 + CHUNKS])

    barrier = pltpu.get_barrier_semaphore()
    peers = [at_z(d) for d in range(1, Z)] + [at_x(d) for d in range(1, X)] + [at_y(d) for d in range(1, Y)] + [sibling]
    for peer in peers:
        pl.semaphore_signal(barrier, inc=1, device_id=peer, device_id_type=MESH)
    load_mid.start()

    @pl.when(z == LAST)
    def _():
        for load in (*load_tail, load_known):
            load.start()

    for load in (load_inv1, load_own, load_here, load_inv0):
        load.start()
    load_mid.wait()
    panel[core, z] = dot(picker(HALF, lambda r: 2 * (r + HALF * core) + 1), mid_raw[...]).astype(BF)
    pl.semaphore_wait(barrier, len(peers))

    def tail_copy(j, d):
        return remote(rhs.at[3, :, side((d - 1) % 2, j)], tail[j].at[y, x], t_send.at[j, d - 1], t_recv.at[j], at_z(d))

    def known_copy(d):
        return remote(rhs.at[2, :, pl.ds((d - 1) % 2 * SIDE, SIDE)], known, k_send.at[d - 1], k_recv, at_z(d))

    def here_copy():
        return remote(rhs.at[:, :, other_side], here.at[odd], h_send, h_recv, partner)

    def panel_copy(d):
        part = panel.at[core, z]
        return remote(part, part, p_send.at[d - 1], p_recv.at[d - 1], at_z(d))

    def panel_share():
        return remote(panel.at[core], panel.at[core], q_send, q_recv, sibling)

    four = pl.ds(4 * core, 4)

    def factor_copy(k):
        shift = {1: -toward, 2: 2 * toward, 3: -3 * toward, 4: toward}[k]
        source = coeffs.at[pl.ds(8 * (turn(shift) // 2) + 4 * core, 4)]
        return remote(source, paired.at[z, four], r_send.at[k - 1], r_recv.at[k - 1], at_z(shift))

    def pass_copy(k):
        part = paired.at[turn(-k * toward), four]
        return remote(part, part, r_send.at[3 + k], r_recv.at[3 + k], partner)

    def share_copy(k):
        part = paired.at[turn(-k * toward if k < 4 else (k - 3) * toward), four]
        return remote(part, part, s_send.at[k - 1], s_recv.at[k - 1], sibling)

    @pl.when(z == LAST)
    def _():
        for j in range(CHUNKS):
            for d in FAR_FIRST:
                tail_copy(j, d).start()

    for d in FAR_FIRST:
        panel_copy(d).start()

    @pl.when(z == LAST)
    def _():
        for d in FAR_FIRST:
            known_copy(d).start()
        for load in (*load_tail, load_known):
            load.wait()

    for k in (4, 1, 2, 3):
        factor_copy(k).start()

    upper, lower = pl.ds(0, HALF), pl.ds(HALF, HALF)

    def gather(which, j, stage, half, d):
        buf = (tail, middle)[which][j]
        send, recv = g_send.at[which, j, stage, half, d - 1], g_recv.at[which, j, stage, half, d - 1]
        if stage == 0:
            part, where = buf.at[y, x, upper if half == 0 else lower], (at_x(d) if half == 0 else at_y(d))
        elif half == 0:
            part, where = buf.at[y, :, upper], at_y(d)
        else:
            part, where = buf.at[:, x, lower], at_x(d)
        return remote(part, part, send, recv, where)

    every = [(half, d) for d in (2, 1, 3) for half in (0, 1)]

    def start(which, j, stage):
        for half, d in every:
            gather(which, j, stage, half, d).start()

    def arrive(which, j, stage):
        for half, d in every:
            gather(which, j, stage, half, d).wait_recv()

    def step(which, j):
        arrive(which, j, 0)
        start(which, j, 1)

    for j in range(CHUNKS):

        @pl.when(z != LAST)
        def _():
            tail_copy(j, 1).wait_recv()

        start(0, j, 0)
    here_copy().start()
    step(0, 0)
    step(0, 1)

    def relay(k):
        factor_copy(k).wait_recv()
        pass_copy(k).start()
        share_copy(k).start()

    for d in FAR_FIRST:
        panel_copy(d).wait_recv()
    panel_share().start()
    load_inv1.wait()

    @pl.when(z != LAST)
    def _():
        known_copy(1).wait_recv()

    panel_share().wait_recv()
    panel_full = jnp.concatenate(
        [jnp.concatenate([panel[v, c] for c in range(Z)], axis=1) for v in range(2)], axis=0
    )

    def solve_last(j):
        arrive(0, j, 1)
        solved = dot(inv[1], tail[j][...].reshape(ORDER, WIDTHS[j])).astype(BF)
        last[j][...] = solved
        part = known[:, STARTS[j] : STARTS[j] + WIDTHS[j]].astype(F32) - dot(panel_full, solved)
        middle[j][y, x] = part.astype(BF)
        start(1, j, 0)

    solve_last(0)
    solve_last(1)
    for k in (1, 2, 3):
        relay(k)
    factor_copy(4).wait_recv()
    share_copy(4).start()
    step(1, 0)
    step(1, 1)
    for k in (1, 2, 3):
        pass_copy(k).wait_recv()
        share_copy(4 + k).start()
    load_own.wait()
    load_here.wait()
    here_copy().wait_recv()
    load_inv0.wait()
    for k in range(1, 8):
        share_copy(k).wait_recv()
    pick = picker(2 * ROWS, lambda r: jnp.where(r < ROWS, 2 * r, 2 * (r - ROWS) + 1))
    for k in range(8):
        both = dot(pick, jnp.concatenate([paired[c, k] for c in range(Z)], axis=1)).astype(BF)
        factor[0, k * ROWS : (k + 1) * ROWS] = both[:ROWS]
        factor[1, k * ROWS : (k + 1) * ROWS] = both[ROWS:]
    for j in range(CHUNKS):
        right = here[:, :, :, STARTS[j] : STARTS[j] + WIDTHS[j]].reshape(8 * ROWS, WIDTHS[j]).astype(F32)
        acc[j][...] = right - dot(factor[1], last[j][...])

    own_rows = pl.ds(pl.multiple_of(row * ROWS, ROWS), ROWS)

    def result_place(j):
        return out.at[:, :, pl.ds(pl.multiple_of(odd * SIDE + STARTS[j], OWN), WIDTHS[j])]

    def keep_copy(j):
        return pltpu.make_async_copy(res[j].at[odd], result_place(j), out_sem.at[j])

    def return_copy(j):
        return remote(res[j].at[1 - odd], result_place(j), o_send.at[j], o_recv.at[j], partner)

    for j in range(CHUNKS):
        arrive(1, j, 1)
        solved = dot(inv[0], middle[j][...].reshape(ORDER, WIDTHS[j])).astype(BF)
        solved_mid[j][...] = solved
        result = (acc[j][...] - dot(factor[0], solved)).astype(BF)
        res[j][...] = result.reshape(2, 4, ROWS, WIDTHS[j])

        @pl.when(z >= LAST - 1)
        def _():
            res[j][1, 2] = solved_mid[j][own_rows]
            res[j][1, 3] = last[j][own_rows]

        return_copy(j).start()
        keep_copy(j).start()

    @pl.when(z == LAST)
    def _():
        for d in FAR_FIRST:
            for j in range(CHUNKS):
                tail_copy(j, d).wait_send()
            known_copy(d).wait_send()

    for d in FAR_FIRST:
        panel_copy(d).wait_send()
    panel_share().wait_send()
    here_copy().wait_send()
    for k in range(1, 8):
        share_copy(k).wait_send()
    for k in range(1, 5):
        factor_copy(k).wait_send()
    for k in range(1, 4):
        pass_copy(k).wait_send()
    for which in range(2):
        for j in range(CHUNKS):
            for stage in range(2):
                for half, d in every:
                    gather(which, j, stage, half, d).wait_send()
    for j in range(CHUNKS):
        keep_copy(j).wait()
        return_copy(j).wait_send()
        remote(res[j].at[odd], out.at[:, :, side(0, j)], o_send.at[j], o_recv.at[j], partner).wait_recv()


def local(coeffs_r, rhs, inverses):
    cycles = coeffs_r.shape[0]
    any_space = pl.BlockSpec(memory_space=pl.ANY)
    dma = pltpu.SemaphoreType.DMA

    def per_chunk(shape, dtype):
        return [pltpu.VMEM((*shape, width), dtype) for width in WIDTHS]

    out = pl.pallas_call(
        kernel,
        out_shape=jax.ShapeDtypeStruct((4, ROWS, 2 * SIDE), BF),
        in_specs=[any_space] * 3,
        out_specs=any_space,
        scratch_shapes=[
            pltpu.VMEM((2, ORDER, ORDER), BF),
            pltpu.VMEM((2, 4, ROWS, SIDE), BF),
            pltpu.VMEM((Z, 8, 2 * ROWS, OWN), BF),
            pltpu.VMEM((2 * ROWS, OWN), BF),
            pltpu.VMEM((2, 8 * ROWS, ORDER), BF),
            pltpu.VMEM((2, Z, HALF, OWN), BF),
            pltpu.VMEM((ROWS, SIDE), BF),
            *per_chunk((Y, X, ROWS), BF),
            *per_chunk((Y, X, ROWS), BF),
            *per_chunk((ORDER,), BF),
            *per_chunk((ORDER,), BF),
            *per_chunk((8 * ROWS,), F32),
            *per_chunk((2, 4, ROWS), BF),
            dma((6 + CHUNKS,)),
            dma((CHUNKS,)),
            dma((CHUNKS, Z - 1)),
            dma((CHUNKS,)),
            dma((Z - 1,)),
            dma,
            dma,
            dma,
            dma((Z - 1,)),
            dma((Z - 1,)),
            dma,
            dma,
            dma((7,)),
            dma((7,)),
            dma((7,)),
            dma((7,)),
            dma((2, CHUNKS, 2, 2, 3)),
            dma((2, CHUNKS, 2, 2, 3)),
            dma((CHUNKS,)),
            dma((CHUNKS,)),
        ],
        compiler_params=pltpu.CompilerParams(
            collective_id=0, has_side_effects=True, vmem_limit_bytes=53 * 1024 * 1024
        ),
    )(
        coeffs_r.reshape(cycles, 2 * ROWS, OWN),
        rhs.reshape(4, ROWS, 2 * SIDE),
        inverses,
    )
    return out.reshape(rhs.shape)


def solution(mesh):
    placed = (P(None, "row", None, None, "col"), P("col", "row", None, "vox"), P())
    return jax.shard_map(
        local, mesh=mesh, in_specs=placed, out_specs=P("col", "row", None, "vox"), check_vma=False
    )
```

time: 55.5 us -> 51.4 us (0.926)
  the two profiles are of different devices: /device:TPU:2 before, /device:TPU:1 now
where the time goes in v2:
time: 51.4 us; the launch traced here: 51.2 us
  Pallas kernels  49.5 us (96%)
  local copies, waits for them, and re-layouts  1.74 us (3%)
    pallas_call x1, Pallas kernels, local(): pl.pallas_call(kernel, out_shape=jax.ShapeDtypeStruct((4, ROWS, 2 * SIDE)...  49.5 us
    unnamed x3, local copies, waits for them, and re-layouts  1.74 us

profile of v2, /device:TPU:1, one launch (start us, length us, event | category | flops | bytes accessed | tf_op | source)
XLA Modules:
  0.0 51.2 jit_solution(14810350996684980934)
XLA Ops:
  0.0 0.0 copy-start
  0.0 1.0 %copy-done = bf16[4,1,64,768]{3,2,1,0:T(8,128)(2,1)S(1)} copy-done((bf16[4,1,64,768]{3,2,1,0:T(8,128)(2,1)S(1)}, bf16[4,1,64,768]{3,2,1,0:T(8,128)(2,1)}, u32[]{:S(2)}) %copy-start) | copy-done | bytes 393240
  1.0 49.5 %shard_map.37 = bf16[4,64,768]{2,1,0:T(8,128)(2,1)S(1)} custom-call(bf16[32,128,128]{2,1,0:T(8,128)(2,1)} %bitcast.7, bf16[4,64,768]{2,1,0:T(8,128)(2,1)S(1)} %bitcast.6, bf16[2,1024,1024]{2,1,0:T(8,128)(2,1)} %inverses.1), custom_call_target="tpu_custom_call" | custom-call | tf_op jit(solution)/shard_map/pallas_call | solution.py:345
  50.5 0.7 %copy.6 = bf16[4,1,64,768]{3,2,1,0:T(8,128)(2,1)} copy(bf16[4,1,64,768]{3,2,1,0:T(8,128)(2,1)S(1)} %bitcast.5) | data formatting | bytes 786432
Async XLA Ops:
  0.0 1.0 %copy-start = (bf16[4,1,64,768]{3,2,1,0:T(8,128)(2,1)S(1)}, bf16[4,1,64,768]{3,2,1,0:T(8,128)(2,1)}, u32[]{:S(2)}) copy-start(bf16[4,1,64,768]{3,2,1,0:T(8,128)(2,1)} %param.4) | copy-start | bytes 1179652

commit v3 on v2

--- a/solution.py
+++ b/solution.py
@@ -19,6 +19,7 @@
 ORDER = 1024
 LAST = Z - 1
 FAR_FIRST = (4, 3, 5, 2, 6, 1, 7)
+FIRST = (2, 6, 1, 7)
 
 
 def dot(a, b):
@@ -145,6 +146,15 @@
     def known_copy(d):
         return remote(rhs.at[2, :, pl.ds((d - 1) % 2 * SIDE, SIDE)], known, k_send.at[d - 1], k_recv, at_z(d))
 
+    passes = (z <= 1, z == LAST - 1)
+    onward = jnp.where(z <= 1, 2, -2)
+
+    def tail_pass(j):
+        return remote(tail[j].at[y, x], tail[j].at[y, x], t_send.at[j, 0], t_recv.at[j], at_z(onward))
+
+    def known_pass():
+        return remote(known, known, k_send.at[0], k_recv, at_z(onward))
+
     def here_copy():
         return remote(rhs.at[:, :, other_side], here.at[odd], h_send, h_recv, partner)
 
@@ -173,7 +183,7 @@
     @pl.when(z == LAST)
     def _():
         for j in range(CHUNKS):
-            for d in FAR_FIRST:
+            for d in FIRST:
                 tail_copy(j, d).start()
 
     for d in FAR_FIRST:
@@ -181,12 +191,12 @@
 
     @pl.when(z == LAST)
     def _():
-        for d in FAR_FIRST:
+        for d in FIRST:
             known_copy(d).start()
         for load in (*load_tail, load_known):
             load.wait()
 
-    for k in (4, 1, 2, 3):
+    for k in (4, 1):
         factor_copy(k).start()
 
     upper, lower = pl.ds(0, HALF), pl.ds(HALF, HALF)
@@ -222,9 +232,22 @@
         def _():
             tail_copy(j, 1).wait_recv()
 
+            @pl.when(jnp.logical_or(*passes))
+            def _():
+                tail_pass(j).start()
+
         start(0, j, 0)
+    for k in (2, 3):
+        factor_copy(k).start()
     here_copy().start()
+
     step(0, 0)
+
+    @pl.when(jnp.logical_or(*passes))
+    def _():
+        known_copy(1).wait_recv()
+        known_pass().start()
+
     step(0, 1)
 
     def relay(k):
@@ -237,7 +260,7 @@
     panel_share().start()
     load_inv1.wait()
 
-    @pl.when(z != LAST)
+    @pl.when(jnp.logical_and(z >= 2, z <= LAST - 2))
     def _():
         known_copy(1).wait_recv()
 
@@ -254,12 +277,13 @@
         middle[j][y, x] = part.astype(BF)
         start(1, j, 0)
 
+    relay(1)
+    factor_copy(4).wait_recv()
+    share_copy(4).start()
     solve_last(0)
     solve_last(1)
-    for k in (1, 2, 3):
-        relay(k)
-    factor_copy(4).wait_recv()
-    share_copy(4).start()
+    relay(2)
+    relay(3)
     step(1, 0)
     step(1, 1)
     for k in (1, 2, 3):
@@ -308,10 +332,16 @@
 
     @pl.when(z == LAST)
     def _():
-        for d in FAR_FIRST:
+        for d in FIRST:
             for j in range(CHUNKS):
                 tail_copy(j, d).wait_send()
             known_copy(d).wait_send()
+
+    @pl.when(jnp.logical_or(*passes))
+    def _():
+        for j in range(CHUNKS):
+            tail_pass(j).wait_send()
+        known_pass().wait_send()
 
     for d in FAR_FIRST:
         panel_copy(d).wait_send()

time: 51.4 us -> 49.5 us (0.963)
  Pallas kernels: 49.5 us -> 47.6 us
    pallas_call x1, Pallas kernels: 49.5 us -> 47.6 us  [local(): pl.pallas_call(kernel, out_shape=jax.ShapeDtypeStruct((4, ROWS, 2 * SIDE)...]
where the time goes in v3:
time: 49.5 us; the launch traced here: 49.4 us
  Pallas kernels  47.6 us (96%)
  local copies, waits for them, and re-layouts  1.74 us (4%)
    pallas_call x1, Pallas kernels, local(): pl.pallas_call(kernel, out_shape=jax.ShapeDtypeStruct((4, ROWS, 2 * SIDE)...  47.6 us
    unnamed x3, local copies, waits for them, and re-layouts  1.74 us

profile of v3, /device:TPU:1, one launch (start us, length us, event | category | flops | bytes accessed | tf_op | source)
XLA Modules:
  0.0 49.4 jit_solution(3535153535929535146)
XLA Ops:
  0.0 0.0 copy-start
  0.0 1.0 %copy-done = bf16[4,1,64,768]{3,2,1,0:T(8,128)(2,1)S(1)} copy-done((bf16[4,1,64,768]{3,2,1,0:T(8,128)(2,1)S(1)}, bf16[4,1,64,768]{3,2,1,0:T(8,128)(2,1)}, u32[]{:S(2)}) %copy-start) | copy-done | bytes 393240
  1.0 47.6 %shard_map.37 = bf16[4,64,768]{2,1,0:T(8,128)(2,1)S(1)} custom-call(bf16[32,128,128]{2,1,0:T(8,128)(2,1)} %bitcast.7, bf16[4,64,768]{2,1,0:T(8,128)(2,1)S(1)} %bitcast.6, bf16[2,1024,1024]{2,1,0:T(8,128)(2,1)} %inverses.1), custom_call_target="tpu_custom_call" | custom-call | tf_op jit(solution)/shard_map/pallas_call | solution.py:375
  48.6 0.7 %copy.6 = bf16[4,1,64,768]{3,2,1,0:T(8,128)(2,1)} copy(bf16[4,1,64,768]{3,2,1,0:T(8,128)(2,1)S(1)} %bitcast.5) | data formatting | bytes 786432
Async XLA Ops:
  0.0 1.0 %copy-start = (bf16[4,1,64,768]{3,2,1,0:T(8,128)(2,1)S(1)}, bf16[4,1,64,768]{3,2,1,0:T(8,128)(2,1)}, u32[]{:S(2)}) copy-start(bf16[4,1,64,768]{3,2,1,0:T(8,128)(2,1)} %param.4) | copy-start | bytes 1179652

commit v4 on v3

--- a/solution.py
+++ b/solution.py
@@ -260,19 +260,21 @@
     panel_share().start()
     load_inv1.wait()
 
-    @pl.when(jnp.logical_and(z >= 2, z <= LAST - 2))
-    def _():
-        known_copy(1).wait_recv()
-
-    panel_share().wait_recv()
-    panel_full = jnp.concatenate(
-        [jnp.concatenate([panel[v, c] for c in range(Z)], axis=1) for v in range(2)], axis=0
-    )
 
     def solve_last(j):
         arrive(0, j, 1)
         solved = dot(inv[1], tail[j][...].reshape(ORDER, WIDTHS[j])).astype(BF)
         last[j][...] = solved
+        if j == 0:
+
+            @pl.when(jnp.logical_and(z >= 2, z <= LAST - 2))
+            def _():
+                known_copy(1).wait_recv()
+
+            panel_share().wait_recv()
+        panel_full = jnp.concatenate(
+            [jnp.concatenate([panel[v, c] for c in range(Z)], axis=1) for v in range(2)], axis=0
+        )
         part = known[:, STARTS[j] : STARTS[j] + WIDTHS[j]].astype(F32) - dot(panel_full, solved)
         middle[j][y, x] = part.astype(BF)
         start(1, j, 0)
@@ -286,23 +288,37 @@
     relay(3)
     step(1, 0)
     step(1, 1)
-    for k in (1, 2, 3):
-        pass_copy(k).wait_recv()
-        share_copy(4 + k).start()
-    load_own.wait()
-    load_here.wait()
-    here_copy().wait_recv()
+    def prepare():
+        for k in (1, 2, 3):
+            pass_copy(k).wait_recv()
+            share_copy(4 + k).start()
+        load_own.wait()
+        load_here.wait()
+        here_copy().wait_recv()
+        for k in range(1, 8):
+            share_copy(k).wait_recv()
+        pick = picker(2 * ROWS, lambda r: jnp.where(r < ROWS, 2 * r, 2 * (r - ROWS) + 1))
+        for k in range(8):
+            both = dot(pick, jnp.concatenate([paired[c, k] for c in range(Z)], axis=1)).astype(BF)
+            factor[0, k * ROWS : (k + 1) * ROWS] = both[:ROWS]
+            factor[1, k * ROWS : (k + 1) * ROWS] = both[ROWS:]
+        for j in range(CHUNKS):
+            right = here[:, :, :, STARTS[j] : STARTS[j] + WIDTHS[j]].reshape(8 * ROWS, WIDTHS[j]).astype(F32)
+            acc[j][...] = right - dot(factor[1], last[j][...])
+
+    def solve_mid(j):
+        arrive(1, j, 1)
+        solved_mid[j][...] = dot(inv[0], middle[j][...].reshape(ORDER, WIDTHS[j])).astype(BF)
+
+    near = jnp.logical_or(z <= 1, z >= 6)
     load_inv0.wait()
-    for k in range(1, 8):
-        share_copy(k).wait_recv()
-    pick = picker(2 * ROWS, lambda r: jnp.where(r < ROWS, 2 * r, 2 * (r - ROWS) + 1))
-    for k in range(8):
-        both = dot(pick, jnp.concatenate([paired[c, k] for c in range(Z)], axis=1)).astype(BF)
-        factor[0, k * ROWS : (k + 1) * ROWS] = both[:ROWS]
-        factor[1, k * ROWS : (k + 1) * ROWS] = both[ROWS:]
-    for j in range(CHUNKS):
-        right = here[:, :, :, STARTS[j] : STARTS[j] + WIDTHS[j]].reshape(8 * ROWS, WIDTHS[j]).astype(F32)
-        acc[j][...] = right - dot(factor[1], last[j][...])
+
+    @pl.when(near)
+    def _():
+        for j in range(CHUNKS):
+            solve_mid(j)
+
+    prepare()
 
     own_rows = pl.ds(pl.multiple_of(row * ROWS, ROWS), ROWS)
 
@@ -316,10 +332,12 @@
         return remote(res[j].at[1 - odd], result_place(j), o_send.at[j], o_recv.at[j], partner)
 
     for j in range(CHUNKS):
-        arrive(1, j, 1)
-        solved = dot(inv[0], middle[j][...].reshape(ORDER, WIDTHS[j])).astype(BF)
-        solved_mid[j][...] = solved
-        result = (acc[j][...] - dot(factor[0], solved)).astype(BF)
+
+        @pl.when(jnp.logical_not(near))
+        def _():
+            solve_mid(j)
+
+        result = (acc[j][...] - dot(factor[0], solved_mid[j][...])).astype(BF)
         res[j][...] = result.reshape(2, 4, ROWS, WIDTHS[j])
 
         @pl.when(z >= LAST - 1)

time: 49.5 us -> 49.3 us (level)
  no operation moved by 1% of the time
where the time goes in v4:
time: 49.3 us; the launch traced here: 49.2 us
  Pallas kernels  47.4 us (96%)
  local copies, waits for them, and re-layouts  1.74 us (4%)
    pallas_call x1, Pallas kernels, local(): pl.pallas_call(kernel, out_shape=jax.ShapeDtypeStruct((4, ROWS, 2 * SIDE)...  47.4 us
    unnamed x3, local copies, waits for them, and re-layouts  1.74 us

profile of v4, /device:TPU:1, one launch (start us, length us, event | category | flops | bytes accessed | tf_op | source)
XLA Modules:
  0.0 49.2 jit_solution(5436311470982378962)
XLA Ops:
  0.0 0.0 copy-start
  0.0 1.0 %copy-done = bf16[4,1,64,768]{3,2,1,0:T(8,128)(2,1)S(1)} copy-done((bf16[4,1,64,768]{3,2,1,0:T(8,128)(2,1)S(1)}, bf16[4,1,64,768]{3,2,1,0:T(8,128)(2,1)}, u32[]{:S(2)}) %copy-start) | copy-done | bytes 393240
  1.0 47.4 %shard_map.37 = bf16[4,64,768]{2,1,0:T(8,128)(2,1)S(1)} custom-call(bf16[32,128,128]{2,1,0:T(8,128)(2,1)} %bitcast.7, bf16[4,64,768]{2,1,0:T(8,128)(2,1)S(1)} %bitcast.6, bf16[2,1024,1024]{2,1,0:T(8,128)(2,1)} %inverses.1), custom_call_target="tpu_custom_call" | custom-call | tf_op jit(solution)/shard_map/pallas_call | solution.py:393
  48.4 0.7 %copy.6 = bf16[4,1,64,768]{3,2,1,0:T(8,128)(2,1)} copy(bf16[4,1,64,768]{3,2,1,0:T(8,128)(2,1)S(1)} %bitcast.5) | data formatting | bytes 786432
Async XLA Ops:
  0.0 1.0 %copy-start = (bf16[4,1,64,768]{3,2,1,0:T(8,128)(2,1)S(1)}, bf16[4,1,64,768]{3,2,1,0:T(8,128)(2,1)}, u32[]{:S(2)}) copy-start(bf16[4,1,64,768]{3,2,1,0:T(8,128)(2,1)} %param.4) | copy-start | bytes 1179652

commit v5 on v4

--- a/solution.py
+++ b/solution.py
@@ -196,8 +196,15 @@
         for load in (*load_tail, load_known):
             load.wait()
 
-    for k in (4, 1):
+    for k in (1, 4):
         factor_copy(k).start()
+    ahead = {2: z == 6, 3: z == 5}
+    for k in (2, 3):
+
+        @pl.when(ahead[k])
+        def _():
+            factor_copy(k).start()
+
 
     upper, lower = pl.ds(0, HALF), pl.ds(HALF, HALF)
 
@@ -237,8 +244,12 @@
                 tail_pass(j).start()
 
         start(0, j, 0)
-    for k in (2, 3):
-        factor_copy(k).start()
+    for k in (3, 2):
+
+        @pl.when(jnp.logical_not(ahead[k]))
+        def _():
+            factor_copy(k).start()
+
     here_copy().start()
 
     step(0, 0)

time: 49.3 us -> 49.3 us (level)
  no operation moved by 1% of the time
where the time goes in v5:
time: 49.3 us; the launch traced here: 49.2 us
  Pallas kernels  47.4 us (96%)
  local copies, waits for them, and re-layouts  1.74 us (4%)
    pallas_call x1, Pallas kernels, local(): pl.pallas_call(kernel, out_shape=jax.ShapeDtypeStruct((4, ROWS, 2 * SIDE)...  47.4 us
    unnamed x3, local copies, waits for them, and re-layouts  1.74 us

profile of v5, /device:TPU:1, one launch (start us, length us, event | category | flops | bytes accessed | tf_op | source)
XLA Modules:
  0.0 49.2 jit_solution(1946988594640908339)
XLA Ops:
  0.0 0.0 copy-start
  0.0 1.0 %copy-done = bf16[4,1,64,768]{3,2,1,0:T(8,128)(2,1)S(1)} copy-done((bf16[4,1,64,768]{3,2,1,0:T(8,128)(2,1)S(1)}, bf16[4,1,64,768]{3,2,1,0:T(8,128)(2,1)}, u32[]{:S(2)}) %copy-start) | copy-done | bytes 393240
  1.0 47.4 %shard_map.37 = bf16[4,64,768]{2,1,0:T(8,128)(2,1)S(1)} custom-call(bf16[32,128,128]{2,1,0:T(8,128)(2,1)} %bitcast.7, bf16[4,64,768]{2,1,0:T(8,128)(2,1)S(1)} %bitcast.6, bf16[2,1024,1024]{2,1,0:T(8,128)(2,1)} %inverses.1), custom_call_target="tpu_custom_call" | custom-call | tf_op jit(solution)/shard_map/pallas_call | solution.py:404
  48.4 0.7 %copy.6 = bf16[4,1,64,768]{3,2,1,0:T(8,128)(2,1)} copy(bf16[4,1,64,768]{3,2,1,0:T(8,128)(2,1)S(1)} %bitcast.5) | data formatting | bytes 786432
Async XLA Ops:
  0.0 1.0 %copy-start = (bf16[4,1,64,768]{3,2,1,0:T(8,128)(2,1)S(1)}, bf16[4,1,64,768]{3,2,1,0:T(8,128)(2,1)}, u32[]{:S(2)}) copy-start(bf16[4,1,64,768]{3,2,1,0:T(8,128)(2,1)} %param.4) | copy-start | bytes 1179652
